TPU v7x, 32 devices: a whole 2x2x4 slice. The times are simulated.
32 devices in a mesh: grp: 2 (over x), rng: 16 (over z, y, core).
Axes of the slice: x: 2, y: 2, z: 4, core: 2. Of those that a mesh axis runs over, the one named last changes fastest.
Arguments:
- mass: bfloat16 [3072, 8, 128], P(('grp', 'rng')), parts along dimension 0, may hold values from 0.05 to 3, as said below
- classes: int32 [3072, 8], P(('grp', 'rng')), parts along dimension 0, may hold values from 0 to 15
- routes: int32 [3072, 2], P(('grp', 'rng')), parts along dimension 0, may hold values from 0 to 15, all different within a row; in each aligned block of 96 rows (0 to 95, 96 to 191, ...) at most 12 rows name the same one
- beam_weight: bfloat16 [256, 256, 1536], P(('grp', 'rng')), parts along dimension 0, may hold values from 0.0001296997 to 0.0012969971
- vertical_weight: bfloat16 [256, 256, 128], P(('grp', 'rng')), parts along dimension 0, may hold values from 0.0003828125 to 0.02890625, as said below
- ray_site: int32 [512], P('grp'), parts along dimension 0, may hold values from 0 to 7
- fit_table: float32 [16, 6], replicated, may hold values from 0.5 to 2
- site_phase: float32 [16], P('grp'), parts along dimension 0, may hold values from -1 to 1
Outputs:
- reflectivity: float32 [256, 256], P(('grp', 'rng')), parts along dimension 0
- phase: float32 [256, 256], P(('grp', 'rng')), parts along dimension 0
There are 2 independent parts, one for each index of `grp`. A program takes and returns all parts, laid end to end along the dimension named above; an argument that names none is the same for every part. Nothing has to cross between parts.
Inputs may be any that keep to these rules, and one draw needn't show every extreme that they name: `routes`: among the rows of one device (96 aligned rows), no gate owner is named more than 12 times, and some gate owner is named exactly 12 times; the 2 entries of a row differ. Every mass content is positive. `vertical_weight`: every level weight is positive.
All inputs are finite; a program needn't handle non-finite values.
Results may differ from a plain program's by a relative error of at most 0.0004.
Values may be sent and summed in bfloat16 or wider, within the bound.
A program may use at most 64 MiB of HBM per device.

v0:
```python
import jax
import jax.numpy as jnp
from jax import lax
from jax.sharding import PartitionSpec as P


def carried_in(value, axis, join, neutral):
    count, mine = (lax.axis_size(axis), lax.axis_index(axis))
    pieces = jax.tree.map(lambda part: lax.all_gather(part, axis), value)
    subtotal = jax.tree.map(
        lambda part, zero: jnp.full_like(part, 0) + jnp.asarray(zero, part.dtype), value, neutral
    )

    def step(position, subtotal):
        longer = join(subtotal, jax.tree.map(lambda part: part[position], pieces))
        return jax.tree.map(lambda new, old: jnp.where(position < mine, new, old), longer, subtotal)

    return lax.fori_loop(0, count - 1, step, subtotal)


def scatter_fit(mass_values, class_onehot, fit_table):
    coeffs = jnp.sum(class_onehot[..., None] * fit_table, axis=-2)
    positive = mass_values > 0
    safe_mass = jnp.where(positive, mass_values, 1.0)
    log_mass = jnp.log(safe_mass)[..., None, :]
    prefactor = coeffs[..., 0::2][..., None]
    exponent = coeffs[..., 1::2][..., None]
    channels = prefactor * jnp.exp(exponent * log_mass)
    channels = jnp.where(positive[..., None, :], channels, 0.0)
    return channels.reshape(channels.shape[:-2] + (3 * channels.shape[-1],))


def add_pairs(earlier, later):
    return (earlier[0] + later[0], earlier[1] + later[1])


def local(mass, classes, routes, beam_weight, vertical_weight, ray_site, fit_table, site_phase):
    devices = lax.axis_size("rng")
    blk_rows, fanout = routes.shape
    columns = mass.shape[1]
    levels = mass.shape[2]
    gate_rows, ray_count, slot_cols = beam_weight.shape
    capacity = slot_cols // (devices * columns)
    table_rows = fit_table.shape[0]
    pair_count = blk_rows * fanout
    targets = routes.reshape(pair_count)
    target_hot = (targets[:, None] == jnp.arange(devices, dtype=jnp.int32)[None, :]).astype(
        jnp.int32
    )
    position = jnp.sum((jnp.cumsum(target_hot, axis=0) - target_hot) * target_hot, axis=1)
    row_of = jnp.arange(pair_count, dtype=jnp.int32) // fanout
    class_onehot = (classes[..., None] == jnp.arange(table_rows, dtype=jnp.int32)).astype(
        jnp.float32
    )
    fields = scatter_fit(mass.astype(jnp.float32), class_onehot, fit_table).astype(jnp.bfloat16)
    outgoing = jnp.zeros((devices, capacity, columns, 3 * levels), jnp.bfloat16)
    outgoing = outgoing.at[targets, position].set(fields[row_of])
    received = lax.all_to_all(outgoing, "rng", split_axis=0, concat_axis=0, tiled=True)
    cells = gate_rows * ray_count
    received = received.reshape(devices * capacity * columns, 3 * levels)
    sampled = jnp.dot(
        beam_weight.reshape(cells, slot_cols), received, preferred_element_type=jnp.float32
    )
    sampled = sampled.reshape(cells, 3, levels)
    beams = jnp.sum(
        sampled * vertical_weight.reshape(cells, levels).astype(jnp.float32)[:, None, :], axis=-1
    )
    beams = beams.reshape(gate_rows, ray_count, 3)
    refl_lin = beams[..., 0]
    atten = beams[..., 1]
    spec_phase = beams[..., 2]
    atten_total = jnp.sum(atten, axis=0)
    phase_total = jnp.sum(spec_phase, axis=0)
    empty = jnp.zeros((ray_count,), jnp.float32)
    atten_before, phase_before = carried_in(
        (atten_total, phase_total), "rng", add_pairs, (empty, empty)
    )
    step_len = 4.0 / (devices * gate_rows)
    depth = step_len * (atten_before[None, :] + jnp.cumsum(atten, axis=0) - 0.5 * atten)
    reflectivity = jnp.log(refl_lin) - 2.0 * depth
    site_count = site_phase.shape[0]
    offsets = jnp.sum(
        (ray_site[:, None] == jnp.arange(site_count, dtype=jnp.int32)[None, :]).astype(jnp.float32)
        * site_phase[None, :],
        axis=1,
    )
    phase = (
        2.0 * step_len * (phase_before[None, :] + jnp.cumsum(spec_phase, axis=0)) + offsets[None, :]
    )
    return (reflectivity, phase)


def solution(mesh):
    placed = (
        P(("grp", "rng"), None, None),
        P(("grp", "rng"), None),
        P(("grp", "rng"), None),
        P(("grp", "rng"), None, None),
        P(("grp", "rng"), None, None),
        P("grp"),
        P(),
        P("grp"),
    )
    return jax.shard_map(
        local,
        mesh=mesh,
        in_specs=placed,
        out_specs=(P(("grp", "rng"), None), P(("grp", "rng"), None)),
        check_vma=False,
    )
```

profile of v0, /device:TPU:0, one launch (start us, length us, event | category | flops | bytes accessed | tf_op | source)
XLA Modules:
  0.0 114.7 jit_solution(13158821820774940830)
XLA Ops:
  0.6 0.8 copy.27
  1.4 0.1 eq.52
  1.5 0.1 reshape.150
  1.7 0.7 fusion.2
  2.4 0.8 multiply_reduce_fusion.1
  3.3 1.0 fusion.1
  4.3 1.0 convert_compare_fusion
  5.3 0.6 reduce-window.6
  5.9 0.2 slice_reduce_fusion
  6.1 0.1 bitcast_bitcast_fusion
  6.2 0.1 copy.31
  6.4 0.1 copy.32
  6.5 0.8 fusion
  7.3 1.0 gather_fusion
  8.3 1.1 broadcast_in_dim.16
  9.5 24.8 %scatter_fusion = bf16[16,12,8,384]{3,2,1,0:T(8,128)(2,1)} fusion(bf16[16,12,8,384]{3,2,1,0:T(8,128)(2,1)} %broadcast_in_dim.16, s32[192]{0:T(256)S(1)} %bitcast.57, bf16[192,8,384]{2,1,0:T(8,128)(2,1)S(1)} %gather_fusion), kind=kCustom, calls=%fused_computation.1 | custom fusion | bytes 3540480 | tf_op jit(solution)/shard_map/scatter | solution.py:57
  34.2 0.0 copy-start
  34.2 7.5 %all-to-all-start = ((bf16[16,12,8,384]{3,2,1,0:T(8,128)(2,1)}), bf16[16,12,8,384]{3,2,1,0:T(8,128)(2,1)S(1)}, u32[]{:S(2)}, u32[]{:S(2)}) async-start(bf16[16,12,8,384]{3,2,1,0:T(8,128)(2,1)} %scatter_fusion), calls=%async_computation | async-start | bytes 2359296 | tf_op jit(solution)/shard_map/all_to_all | solution.py:58
  41.8 0.0 copy-done
  41.8 0.1 bitcast_convert_fusion
  41.9 0.0 copy-start.1
  42.0 0.0 copy-start.2
  42.0 0.3 copy.33
  42.3 0.3 copy-done.1
  42.6 0.0 copy-done.2
  42.6 0.1 select_reduce_fusion
  42.7 24.2 %all-to-all-done = bf16[16,12,8,384]{3,2,1,0:T(8,128)(2,1)S(1)} async-done(((bf16[16,12,8,384]{3,2,1,0:T(8,128)(2,1)}), bf16[16,12,8,384]{3,2,1,0:T(8,128)(2,1)S(1)}, u32[]{:S(2)}, u32[]{:S(2)}) %all-to-all-start) | async-done | bytes 1179680 | tf_op jit(solution)/shard_map/all_to_all | solution.py:58
  66.9 4.9 %fusion.8 = f32[384,2048]{1,0:T(8,128)S(1)} fusion(bf16[1536,384]{1,0:T(8,128)(2,1)S(1)} %bitcast.59, bf16[2048,1536]{1,0:T(8,128)(2,1)} %bitcast.71), kind=kOutput, calls=%fused_computation.51 | convolution fusion | flops 2415919104 | bytes 10616832 | tf_op jit(solution)/shard_map/dot_general | solution.py:61
  71.8 0.4 multiply_reduce_fusion
  72.3 23.2 %all-gather.3 = f32[16,1,256]{2,1,0:T(1,128)S(1)} all-gather(f32[1,1,256]{2,1,0:T(1,128)S(1)} %bitcast.69), channel_id=3, replica_groups=mesh['grp'=2,'rng'=16] {'rng'}, dimensions={0}, use_global_device_ids=true | all-gather | bytes 17408 | tf_op jit(solution)/shard_map/all_gather | solution.py:9
  95.5 17.4 %all-gather.2 = f32[16,1,256]{2,1,0:T(1,128)S(1)} all-gather(f32[1,1,256]{2,1,0:T(1,128)S(1)} %bitcast.68), channel_id=2, replica_groups=mesh['grp'=2,'rng'=16] {'rng'}, dimensions={0}, use_global_device_ids=true | all-gather | bytes 17408 | tf_op jit(solution)/shard_map/all_gather | solution.py:9
  112.9 1.1 while.16
  114.0 0.6 fusion.6
  (63 shorter events, 0.8 us)
Async XLA Ops:
  34.2 7.6 %copy-start = (bf16[8,256,128]{2,1,0:T(8,128)(2,1)S(1)}, bf16[8,256,128]{2,1,0:T(8,128)(2,1)}, u32[]{:S(2)}) copy-start(bf16[8,256,128]{2,1,0:T(8,128)(2,1)} %param.14) | copy-start | bytes 1572868
  34.2 32.7 %all-to-all-start = ((bf16[16,12,8,384]{3,2,1,0:T(8,128)(2,1)}), bf16[16,12,8,384]{3,2,1,0:T(8,128)(2,1)S(1)}, u32[]{:S(2)}, u32[]{:S(2)}) async-start(bf16[16,12,8,384]{3,2,1,0:T(8,128)(2,1)} %scatter_fusion), calls=%async_computation | async-start | bytes 2359296 | tf_op jit(solution)/shard_map/all_to_all | solution.py:58
  41.9 0.7 copy-start.1
  42.0 0.7 copy-start.2
where the time goes:
time: 116 us; the launch traced here: 115 us
  blocking collectives  40.6 us (35%)
  local copies, waits for them, and re-layouts  29.4 us (25%)
  waiting for transfers between devices  24.2 us (21%)
  starting transfers between devices  7.55 us (7%)
  other arithmetic  6.58 us (6%)
  matrix products  4.86 us (4%)
    all_gather x2, blocking collectives, carried_in(): pieces = jax.tree.map(lambda part: lax.all_gather(part, axis), value)  40.6 us
    scatter x1, local copies, waits for them, and re-layouts, local(): outgoing = outgoing.at[targets, position].set(fields[row_of])  24.8 us
    all_to_all x1, waiting for transfers between devices, local(): lax.all_to_all(outgoing, 'rng', split_axis=0, concat_axis=0, tiled=True)  24.2 us
    all_to_all x1, starting transfers between devices, local(): lax.all_to_all(outgoing, 'rng', split_axis=0, concat_axis=0, tiled=True)  7.55 us
    dot_general x1, matrix products, local(): jnp.dot(beam_weight.reshape(cells, slot_cols), received, preferred_elemen...  4.86 us
  transfers between devices with their start and end apart: 1, of which 1 were waited for; matrix products, arithmetic and copies ran while one was open for 0% of the time, Pallas kernels for 0%

commit v1 on v0

v1 whole, which is shorter than its diff:
```python
import functools

import jax
import jax.numpy as jnp
from jax import lax
from jax.experimental import pallas as pl
from jax.experimental.pallas import tpu as pltpu
from jax.sharding import PartitionSpec as P

MESH = pl.DeviceIdType.MESH
BF16, F32 = jnp.bfloat16, jnp.float32
PLANES = 4


def iota(shape, dim):
    return lax.broadcasted_iota(jnp.int32, shape, dim)


def block_of(index, size):
    return jnp.floor((index.astype(F32) + 0.5) * (1.0 / size))


def dot(a, b, contract=((1,), (0,)), precision=None):
    return lax.dot_general(
        a, b, (contract, ((), ())), preferred_element_type=F32, precision=precision
    )


def kernel(
    n, cap,
    mass_ref, classes_ref, routes_ref, ray_ref, table_ref, site_ref, weight_hbm, vertical_hbm,
    refl_ref, phase_ref,
    weight, vertical, vertical_t, mass_f32, slots_f32, out_mass, out_class, in_mass, in_class,
    out_total, in_total, beam_acc, load_sem, send_sem, recv_sem,
):
    me = lax.axis_index("rng")
    blocks, cols, levels = mass_ref.shape
    gates, rays = refl_ref.shape
    members = n // PLANES
    chunk = cap * cols
    depth = members * chunk
    slots = n * cap
    plane, place = me // members, me % members
    half = plane // 2

    def to(rank):
        return {"rng": rank}

    barrier = pltpu.get_barrier_semaphore()

    def greet(i, _):
        pl.semaphore_signal(barrier, 1, device_id=to((me + i) % n), device_id_type=MESH)
        return 0

    lax.fori_loop(1, n, greet, 0)

    def weight_load(z):
        return pltpu.make_async_copy(
            weight_hbm.at[:, pl.ds(z * depth, depth)], weight.at[z], load_sem.at[z]
        )

    vertical_load = pltpu.make_async_copy(vertical_hbm, vertical, load_sem.at[PLANES])
    vertical_load.start()
    for z in range(PLANES):
        weight_load(z).start()

    owner = iota((blocks, n), 1)
    named = (routes_ref[:, 0:1] == owner) | (routes_ref[:, 1:2] == owner)
    earlier = (iota((blocks, blocks), 1) < iota((blocks, blocks), 0)).astype(F32).astype(BF16)
    position = dot(earlier, named.astype(F32).astype(BF16))
    position = jnp.where(named, position, -1.0).astype(BF16)
    slot_lane = iota((n, slots), 1)
    first = iota((n, slots), 0) * cap
    spread = ((slot_lane >= first) & (slot_lane < first + cap)).astype(F32).astype(BF16)
    lane = iota((blocks, slots), 1)
    lane_position = lane.astype(F32) - cap * block_of(lane, cap)
    fills = (dot(position, spread) == lane_position).astype(F32).astype(BF16)

    mass_f32[...] = mass_ref[...].astype(F32).reshape(blocks * cols, levels)
    by_block = jnp.concatenate(
        [mass_f32[pl.ds(c, blocks, stride=cols), :].astype(BF16) for c in range(cols)], axis=1
    )
    picked = dot(fills, by_block, ((0,), (0,)))
    for c in range(cols):
        slots_f32[pl.ds(c, slots, stride=cols), :] = picked[:, c * levels : (c + 1) * levels]
    out_mass[...] = slots_f32[...].astype(BF16).reshape(n, chunk, levels)

    tile = iota((cols, 128), 1)
    tile_col = tile.astype(F32) - cols * block_of(tile, cols)
    tile = (tile_col == iota((cols, 128), 0).astype(F32)).astype(F32).astype(BF16)
    class_tiles = dot(classes_ref[...].astype(F32).astype(BF16), tile).astype(BF16)
    slot_class = dot(fills, class_tiles, ((0,), (0,)))
    row = iota((slots, 128), 0)
    row_position = row.astype(F32) - cap * block_of(row, cap)
    own_lanes = block_of(iota((slots, 128), 1), cols) == row_position
    class_rows = dot(spread, jnp.where(own_lanes, slot_class, 0.0).astype(BF16))
    out_class[...] = class_rows.reshape(n, 1, 128)

    def mass_copy(target, source):
        return pltpu.make_async_remote_copy(
            src_ref=out_mass.at[target], dst_ref=in_mass.at[source],
            send_sem=send_sem.at[0, target], recv_sem=recv_sem.at[0, source],
            device_id=to(target), device_id_type=MESH,
        )

    def class_copy(target, source):
        return pltpu.make_async_remote_copy(
            src_ref=out_class.at[target], dst_ref=in_class.at[source],
            send_sem=send_sem.at[1, target], recv_sem=recv_sem.at[1, source],
            device_id=to(target), device_id_type=MESH,
        )

    def total_copy(target, source):
        return pltpu.make_async_remote_copy(
            src_ref=out_total, dst_ref=in_total.at[source],
            send_sem=send_sem.at[2, target], recv_sem=recv_sem.at[2, source],
            device_id=to(target), device_id_type=MESH,
        )

    near = plane + 1 - 2 * (plane % 2)
    far, farthest = 2 - half, 3 - 3 * half

    def each(z, start, act):
        def step(i, _):
            act(z * members + (place + i) % members)
            return 0

        lax.fori_loop(start, members, step, 0)

    def send(target):
        class_copy(target, me).start()
        mass_copy(target, me).start()

    def arrive(source):
        class_copy(source, source).wait_recv()
        mass_copy(source, source).wait_recv()

    pl.semaphore_wait(barrier, n - 1)
    each(farthest, 0, send)
    each(far, 0, send)
    each(near, 0, send)
    each(plane, 1, send)

    in_mass[me] = out_mass[me]
    in_class[me] = out_class[me]

    vertical_load.wait()
    vertical_t[...] = vertical[...].astype(F32).T
    for z in range(PLANES):
        weight_load(z).wait()

    lane = iota((chunk, depth), 1)
    lane_place = block_of(lane, chunk)
    unroll = (lane.astype(F32) - chunk * lane_place == iota((chunk, depth), 0).astype(F32))
    unroll = unroll.astype(F32).astype(BF16)
    from_place = block_of(iota((members, depth), 1), chunk) == iota((members, depth), 0).astype(F32)

    def absorb(z, initial):
        chosen = pl.ds(z * members, members)
        class_grid = in_class[chosen].reshape(members, 128)[:, :chunk].astype(BF16)
        class_row = jnp.sum(jnp.where(from_place, dot(class_grid, unroll), 0.0), axis=0, keepdims=True)
        onehot = (class_row == iota((table_ref.shape[0], depth), 0).astype(F32)).astype(F32)
        coeffs = dot(table_ref[...], onehot, ((0,), (0,)), lax.Precision.HIGHEST)
        mass_t = in_mass[chosen].reshape(depth, levels).astype(F32).T
        positive = mass_t > 0
        log_mass = jnp.log2(jnp.where(positive, mass_t, 1.0))
        fields_t = jnp.concatenate(
            [
                jnp.where(
                    positive,
                    coeffs[2 * j : 2 * j + 1] * jnp.exp2(coeffs[2 * j + 1 : 2 * j + 2] * log_mass),
                    0.0,
                ).astype(BF16)
                for j in range(3)
            ],
            axis=0,
        )
        for g in range(gates):
            cells = slice(g * rays, (g + 1) * rays)
            sampled = dot(fields_t, weight[z, cells, :], ((1,), (1,)))
            v = vertical_t[:, cells]
            for j in range(3):
                part = sampled[j * levels : (j + 1) * levels] * v
                part = jnp.sum(part.reshape(levels // 8, 8, rays), axis=0)
                if initial:
                    beam_acc[j, :, cells] = part
                else:
                    beam_acc[j, :, cells] += part

    each(plane, 1, arrive)
    absorb(plane, True)
    each(near, 0, arrive)
    absorb(near, False)
    each(far, 0, arrive)
    absorb(far, False)
    each(farthest, 0, arrive)
    absorb(farthest, False)

    gate_row = iota((gates, rays), 0)

    def gate_rows(j):
        rows = jnp.zeros((gates, rays), F32)
        for g in range(gates):
            beam = jnp.sum(beam_acc[j, :, g * rays : (g + 1) * rays], axis=0, keepdims=True)
            rows = jnp.where(gate_row == g, beam, rows)
        return rows

    atten, spec_phase = gate_rows(1), gate_rows(2)
    out_total[0:1, :] = jnp.sum(atten, axis=0, keepdims=True)
    out_total[1:2, :] = jnp.sum(spec_phase, axis=0, keepdims=True)

    def send_total(target):
        total_copy(target, me).start()

    for z, start in ((farthest, 0), (far, 0), (near, 0), (plane, 1)):
        each(z, start, send_total)

    def running(rows):
        sums = jnp.zeros((gates, rays), F32)
        for g in range(gates):
            sums = sums + jnp.where(gate_row >= g, rows[g : g + 1], 0.0)
        return sums

    log_refl = jnp.log(gate_rows(0))
    atten_depth = running(atten) - 0.5 * atten
    phase_sum = running(spec_phase)
    offsets = jnp.zeros((1, rays), F32)
    for i in range(site_ref.shape[1]):
        offsets = offsets + jnp.where(ray_ref[...] == i, site_ref[0, i], 0.0)

    for z, start in ((plane, 1), (near, 0), (far, 0), (farthest, 0)):
        each(z, start, lambda source: total_copy(source, source).wait_recv())

    in_total[me] = out_total[...]
    sources = in_total[...]
    before = jnp.sum(jnp.where(iota(sources.shape, 0) < me, sources, 0.0), axis=0)
    step_len = 4.0 / (n * gates)
    refl_ref[...] = log_refl - 2.0 * step_len * (before[0:1] + atten_depth)
    phase_ref[...] = 2.0 * step_len * (before[1:2] + phase_sum) + offsets

    def sent(target):
        class_copy(target, me).wait_send()
        mass_copy(target, me).wait_send()
        total_copy(target, me).wait_send()

    for z, start in ((plane, 1), (near, 0), (far, 0), (farthest, 0)):
        each(z, start, sent)


def local(mass, classes, routes, beam_weight, vertical_weight, ray_site, fit_table, site_phase):
    n = lax.axis_size("rng")
    blocks, cols, levels = mass.shape
    gates, rays, slot_cols = beam_weight.shape
    cap = slot_cols // (n * cols)
    cells = gates * rays
    chunk = cap * cols
    vmem, hbm = pl.BlockSpec(memory_space=pltpu.VMEM), pl.BlockSpec(memory_space=pl.ANY)
    smem = pl.BlockSpec(memory_space=pltpu.SMEM)
    return pl.pallas_call(
        functools.partial(kernel, n, cap),
        out_shape=(jax.ShapeDtypeStruct((gates, rays), F32),) * 2,
        in_specs=[vmem, vmem, vmem, vmem, vmem, smem, hbm, hbm],
        out_specs=(vmem, vmem),
        scratch_shapes=[
            pltpu.VMEM((PLANES, cells, slot_cols // PLANES), BF16),
            pltpu.VMEM((cells, levels), BF16),
            pltpu.VMEM((levels, cells), F32),
            pltpu.VMEM((blocks * cols, levels), F32),
            pltpu.VMEM((slot_cols, levels), F32),
            pltpu.VMEM((n, chunk, levels), BF16),
            pltpu.VMEM((n, 1, 128), F32),
            pltpu.VMEM((n, chunk, levels), BF16),
            pltpu.VMEM((n, 1, 128), F32),
            pltpu.VMEM((2, rays), F32),
            pltpu.VMEM((n, 2, rays), F32),
            pltpu.VMEM((3, 8, cells), F32),
            pltpu.SemaphoreType.DMA((PLANES + 1,)),
            pltpu.SemaphoreType.DMA((3, n)),
            pltpu.SemaphoreType.DMA((3, n)),
        ],
        compiler_params=pltpu.CompilerParams(
            collective_id=0, has_side_effects=True, vmem_limit_bytes=56 * 1024 * 1024
        ),
    )(
        mass, classes, routes, ray_site.reshape(1, rays), fit_table, site_phase.reshape(1, -1),
        beam_weight.reshape(cells, slot_cols), vertical_weight.reshape(cells, levels),
    )


def solution(mesh):
    placed = (
        P(("grp", "rng"), None, None),
        P(("grp", "rng"), None),
        P(("grp", "rng"), None),
        P(("grp", "rng"), None, None),
        P(("grp", "rng"), None, None),
        P("grp"),
        P(),
        P("grp"),
    )
    return jax.shard_map(
        local,
        mesh=mesh,
        in_specs=placed,
        out_specs=(P(("grp", "rng"), None), P(("grp", "rng"), None)),
        check_vma=False,
    )
```

time: 116 us -> 33.1 us (0.29)
  blocking collectives: 40.6 us -> 0 us
  Pallas kernels: 0 us -> 25.3 us
  waiting for transfers between devices: 24.2 us -> 0 us
  local copies, waits for them, and re-layouts: 29.4 us -> 6.73 us
  starting transfers between devices: 7.55 us -> 0 us
  other arithmetic: 6.58 us -> 0 us
  matrix products: 4.86 us -> 0 us
    all_gather x2 -> x0, blocking collectives: 40.6 us -> none  [carried_in(): pieces = jax.tree.map(lambda part: lax.all_gather(part, axis), value)]
    pallas_call x0 -> x1, Pallas kernels: none -> 25.3 us  [local(): pl.pallas_call(functools.partial(kernel, n, cap), out_shape=(jax.ShapeDty...]
    scatter x1 -> x0, local copies, waits for them, and re-layouts: 24.8 us -> none  [local(): outgoing = outgoing.at[targets, position].set(fields[row_of])]
    all_to_all x1 -> x0, waiting for transfers between devices: 24.2 us -> none  [local(): lax.all_to_all(outgoing, 'rng', split_axis=0, concat_axis=0, tiled=True)]
    all_to_all x1 -> x0, starting transfers between devices: 7.55 us -> none  [local(): lax.all_to_all(outgoing, 'rng', split_axis=0, concat_axis=0, tiled=True)]
    unnamed x10 -> x5, local copies, waits for them, and re-layouts: 1.12 us -> 6.73 us
    dot_general x1 -> x0, matrix products: 4.86 us -> none  [local(): jnp.dot(beam_weight.reshape(cells, slot_cols), received, preferred_elemen...]
    reduce_sum x5 -> x0, other arithmetic: 1.39 us -> none  [the longest x1 0.83 us: scatter_fit(): coeffs = jnp.sum(class_onehot[..., None] * fit_table, axis=-2)]
  transfers between devices with their start and end apart: 1 -> 0, of which waited for: 1 -> 0; matrix products, arithmetic and copies ran while one was open for 0% -> 0% of each run, Pallas kernels for 0% -> 0%
where the time goes in v1:
time: 33.1 us; the launch traced here: 32.7 us
  Pallas kernels  25.3 us (76%)
  local copies, waits for them, and re-layouts  6.73 us (20%)
  between operations  0.64 us (2%)
    pallas_call x1, Pallas kernels, local(): pl.pallas_call(functools.partial(kernel, n, cap), out_shape=(jax.ShapeDty...  25.3 us
    unnamed x5, local copies, waits for them, and re-layouts  6.73 us

profile of v1, /device:TPU:0, one launch (start us, length us, event | category | flops | bytes accessed | tf_op | source)
XLA Modules:
  0.0 32.7 jit_solution(12123933384291820788)
XLA Ops:
  0.6 1.4 %copy.12.table_ref = f32[16,6]{1,0:T(8,128)} copy(f32[16,6]{0,1:T(8,128)} %param.14) | data formatting | bytes 768 | tf_op args[6]
  2.0 1.4 %copy.10.classes_ref = s32[96,8]{1,0:T(8,128)} copy(s32[96,8]{0,1:T(8,128)} %param.9) | data formatting | bytes 6144 | tf_op args[1]
  3.4 1.4 %copy.11.routes_ref = s32[96,2]{1,0:T(8,128)} copy(s32[96,2]{0,1:T(2,128)} %param.10) | data formatting | bytes 1536 | tf_op args[2]
  4.8 25.3 %shard_map.95 = (f32[8,256]{1,0:T(8,128)}, f32[8,256]{1,0:T(8,128)}) custom-call(bf16[96,8,128]{2,1,0:T(8,128)(2,1)} %mass_ref.1, s32[96,8]{1,0:T(8,128)} %copy.10.classes_ref, s32[96,2]{1,0:T(8,128)} %copy.11.routes_ref, s32[1,256]{1,0:T(1,128)} %bitcast.6, f32[16,6]{1,0:T(8,128)} %copy.12.table_ref, f32[1,8]{1,0:T(1,128)} %bitcast.7, ...), custom_call_target="tpu_custom_call" | custom-call | tf_op jit(solution)/shard_map/pallas_call | solution.py:259
  30.1 1.3 %copy.15 = f32[8,256]{1,0:T(8,128)} copy(f32[8,256]{1,0:T(8,128)} %get-tuple-element.4) | data formatting | bytes 16384
  31.4 1.3 %copy.16 = f32[8,256]{1,0:T(8,128)} copy(f32[8,256]{1,0:T(8,128)} %get-tuple-element.5) | data formatting | bytes 16384

commit v2 on v1

v2 whole, which is shorter than its diff:
```python
import functools

import jax
import jax.numpy as jnp
from jax import lax
from jax.experimental import pallas as pl
from jax.experimental.pallas import tpu as pltpu
from jax.sharding import PartitionSpec as P

MESH = pl.DeviceIdType.MESH
BF16, F32 = jnp.bfloat16, jnp.float32
PLANES = 4


def iota(shape, dim):
    return lax.broadcasted_iota(jnp.int32, shape, dim)


def block_of(index, size):
    return jnp.floor((index.astype(F32) + 0.5) * (1.0 / size))


def dot(a, b, contract=((1,), (0,)), precision=None):
    return lax.dot_general(
        a, b, (contract, ((), ())), preferred_element_type=F32, precision=precision
    )


def kernel(
    n, cap,
    mass_hbm, classes_hbm, routes_hbm, ray_hbm, table_hbm, site_hbm, weight_hbm, vertical_hbm,
    refl_ref, phase_ref,
    mass_ref, classes_ref, routes_ref, ray_ref, table_ref, site_ref,
    weight, vertical, vertical_t, mass_f32, slots_f32, out_mass, out_class, in_mass, in_class,
    out_total, in_total, beam_acc, load_sem, send_sem, mass_sem, class_sem, total_sem,
):
    me = lax.axis_index("rng")
    blocks, cols, levels = mass_ref.shape
    gates, rays = refl_ref.shape
    members = n // PLANES
    chunk = cap * cols
    depth = members * chunk
    slots = n * cap
    plane, place = me // members, me % members
    half = plane // 2

    def to(rank):
        return {"rng": rank}

    barrier = pltpu.get_barrier_semaphore()

    def greet(i, _):
        pl.semaphore_signal(barrier, 1, device_id=to((me + i) % n), device_id_type=MESH)
        return 0

    lax.fori_loop(1, n, greet, 0, unroll=n <= 16)

    small = [
        pltpu.make_async_copy(source, target, load_sem.at[PLANES + 1 + i])
        for i, (source, target) in enumerate(
            (
                (routes_hbm, routes_ref),
                (mass_hbm, mass_ref),
                (classes_hbm, classes_ref),
                (table_hbm, table_ref),
                (ray_hbm, ray_ref),
                (site_hbm, site_ref),
            )
        )
    ]
    for copy in small:
        copy.start()

    def weight_load(z):
        return pltpu.make_async_copy(
            weight_hbm.at[:, pl.ds(z * depth, depth)], weight.at[z], load_sem.at[z]
        )

    vertical_load = pltpu.make_async_copy(vertical_hbm, vertical, load_sem.at[PLANES])
    vertical_load.start()
    for z in range(PLANES):
        weight_load(z).start()

    for copy in small[:3]:
        copy.wait()

    owner = iota((n, blocks), 0)
    named = (routes_ref[0:1, :] == owner) | (routes_ref[1:2, :] == owner)
    earlier = (iota((blocks, blocks), 0) < iota((blocks, blocks), 1)).astype(F32).astype(BF16)
    position = dot(named.astype(F32).astype(BF16), earlier)
    position = jnp.where(named, position, -1.0).astype(BF16)
    row = iota((slots, n), 0).astype(F32)
    owns = (block_of(row, cap) == iota((slots, n), 1).astype(F32)).astype(F32).astype(BF16)
    row = iota((slots, blocks), 0).astype(F32)
    fills = (dot(owns, position) == row - cap * block_of(row, cap)).astype(F32).astype(BF16)

    mass_f32[...] = mass_ref[...].astype(F32).reshape(blocks * cols, levels)
    by_block = jnp.concatenate(
        [mass_f32[pl.ds(c, blocks, stride=cols), :].astype(BF16) for c in range(cols)], axis=1
    )
    picked = dot(fills, by_block)
    for c in range(cols):
        slots_f32[pl.ds(c, slots, stride=cols), :] = picked[:, c * levels : (c + 1) * levels]
    out_mass[...] = slots_f32[...].astype(BF16).reshape(n, chunk, levels)

    slot_class = dot(fills, classes_ref[...].astype(F32).astype(BF16), ((1,), (1,))).astype(BF16)
    tile = iota((cols, 128), 1).astype(F32)
    tile = tile - cols * block_of(tile, cols) == iota((cols, 128), 0).astype(F32)
    row = iota((slots, 128), 0).astype(F32)
    own_lanes = block_of(iota((slots, 128), 1), cols) == row - cap * block_of(row, cap)
    tiled = jnp.where(own_lanes, dot(slot_class, tile.astype(F32).astype(BF16)), 0.0).astype(BF16)
    spread = (block_of(iota((n, slots), 1), cap) == iota((n, slots), 0).astype(F32))
    class_rows = dot(spread.astype(F32).astype(BF16), tiled)
    out_class[...] = class_rows.reshape(n, 1, 128)

    def mass_copy(target):
        return pltpu.make_async_remote_copy(
            src_ref=out_mass.at[target], dst_ref=in_mass.at[me],
            send_sem=send_sem.at[0], recv_sem=mass_sem.at[plane],
            device_id=to(target), device_id_type=MESH,
        )

    def class_copy(target):
        return pltpu.make_async_remote_copy(
            src_ref=out_class.at[target], dst_ref=in_class.at[me],
            send_sem=send_sem.at[1], recv_sem=class_sem.at[plane],
            device_id=to(target), device_id_type=MESH,
        )

    def total_copy(target):
        return pltpu.make_async_remote_copy(
            src_ref=out_total, dst_ref=in_total.at[me],
            send_sem=send_sem.at[2], recv_sem=total_sem,
            device_id=to(target), device_id_type=MESH,
        )

    def wait_bytes(ref, count, sem):
        part = ref.at[pl.ds(0, count)]
        pltpu.make_async_copy(part, part, sem).wait()

    near = plane + 1 - 2 * (plane % 2)
    far, last = (plane + 2) % PLANES, PLANES - 1 - plane
    others = ((last, 0), (far, 0), (near, 0), (plane, 1))

    def each(z, start, act):
        def step(i, _):
            act(z * members + (place + i) % members)
            return 0

        lax.fori_loop(start, members, step, 0, unroll=n <= 16)

    def arrive(z, count):
        wait_bytes(in_class, count, class_sem.at[z])
        wait_bytes(in_mass, count, mass_sem.at[z])

    pl.semaphore_wait(barrier, n - 1)
    for z, start in ((far, 0), (last, 0), (near, 0), (plane, 1)):
        each(z, start, lambda target: mass_copy(target).start())
        each(z, start, lambda target: class_copy(target).start())

    in_mass[me] = out_mass[me]
    in_class[me] = out_class[me]

    for copy in small[3:]:
        copy.wait()
    vertical_load.wait()
    vertical_t[...] = vertical[...].astype(F32).T
    for z in range(PLANES):
        weight_load(z).wait()

    lane = iota((chunk, depth), 1)
    lane_place = block_of(lane, chunk)
    unroll = (lane.astype(F32) - chunk * lane_place == iota((chunk, depth), 0).astype(F32))
    unroll = unroll.astype(F32).astype(BF16)
    from_place = block_of(iota((members, depth), 1), chunk) == iota((members, depth), 0).astype(F32)

    def absorb(z, initial):
        chosen = pl.ds(z * members, members)
        class_grid = in_class[chosen].reshape(members, 128)[:, :chunk].astype(BF16)
        class_row = jnp.sum(jnp.where(from_place, dot(class_grid, unroll), 0.0), axis=0, keepdims=True)
        onehot = (class_row == iota((table_ref.shape[1], depth), 0).astype(F32)).astype(F32)
        coeffs = dot(table_ref[...], onehot, precision=lax.Precision.HIGHEST)
        mass_t = in_mass[chosen].reshape(depth, levels).astype(F32).T
        positive = mass_t > 0
        log_mass = jnp.log2(jnp.where(positive, mass_t, 1.0))
        fields_t = jnp.concatenate(
            [
                jnp.where(
                    positive,
                    coeffs[2 * j : 2 * j + 1] * jnp.exp2(coeffs[2 * j + 1 : 2 * j + 2] * log_mass),
                    0.0,
                ).astype(BF16)
                for j in range(3)
            ],
            axis=0,
        )
        for g in range(gates):
            cells = slice(g * rays, (g + 1) * rays)
            sampled = dot(fields_t, weight[z, cells, :], ((1,), (1,)))
            v = vertical_t[:, cells]
            for j in range(3):
                part = sampled[j * levels : (j + 1) * levels] * v
                part = jnp.sum(part.reshape(levels // 8, 8, rays), axis=0)
                if initial:
                    beam_acc[j, :, cells] = part
                else:
                    beam_acc[j, :, cells] += part

    arrive(plane, members - 1)
    absorb(plane, True)
    for z in (near, far, last):
        arrive(z, members)
        absorb(z, False)

    gate_row = iota((gates, rays), 0)

    def gate_rows(j):
        rows = jnp.zeros((gates, rays), F32)
        for g in range(gates):
            beam = jnp.sum(beam_acc[j, :, g * rays : (g + 1) * rays], axis=0, keepdims=True)
            rows = jnp.where(gate_row == g, beam, rows)
        return rows

    for j in range(2):
        sums = beam_acc[j + 1, :, 0:rays]
        for g in range(1, gates):
            sums = sums + beam_acc[j + 1, :, g * rays : (g + 1) * rays]
        out_total[j : j + 1, :] = jnp.sum(sums, axis=0, keepdims=True)
    for z, start in others:
        each(z, start, lambda target: total_copy(target).start())

    atten, spec_phase = gate_rows(1), gate_rows(2)
    in_total[me] = out_total[...]
    wait_bytes(out_mass, n - 1, send_sem.at[0])
    wait_bytes(out_class, n - 1, send_sem.at[1])

    def running(rows):
        sums = jnp.zeros((gates, rays), F32)
        for g in range(gates):
            sums = sums + jnp.where(gate_row >= g, rows[g : g + 1], 0.0)
        return sums

    log_refl = jnp.log(gate_rows(0))
    atten_depth = running(atten) - 0.5 * atten
    phase_sum = running(spec_phase)
    offsets = jnp.zeros((1, rays), F32)
    for i in range(site_ref.shape[1]):
        offsets = offsets + jnp.where(ray_ref[...] == i, site_ref[0, i], 0.0)

    wait_bytes(in_total, n - 1, total_sem)
    sources = in_total[...]
    before = jnp.sum(jnp.where(iota(sources.shape, 0) < me, sources, 0.0), axis=0)
    step_len = 4.0 / (n * gates)
    refl_ref[...] = log_refl - 2.0 * step_len * (before[0:1] + atten_depth)
    phase_ref[...] = 2.0 * step_len * (before[1:2] + phase_sum) + offsets

    wait_bytes(in_total, n - 1, send_sem.at[2])


def finish(refl_ref, phase_ref, refl_out, phase_out):
    refl_out[...] = refl_ref[...]
    phase_out[...] = phase_ref[...]


def local(mass, classes, routes, beam_weight, vertical_weight, ray_site, fit_table, site_phase):
    n = lax.axis_size("rng")
    blocks, cols, levels = mass.shape
    gates, rays, slot_cols = beam_weight.shape
    cap = slot_cols // (n * cols)
    cells = gates * rays
    chunk = cap * cols
    vmem, hbm = pl.BlockSpec(memory_space=pltpu.VMEM), pl.BlockSpec(memory_space=pl.ANY)
    refl, phase = pl.pallas_call(
        functools.partial(kernel, n, cap),
        out_shape=(jax.ShapeDtypeStruct((gates, rays), F32),) * 2,
        in_specs=[hbm] * 8,
        out_specs=(vmem, vmem),
        scratch_shapes=[
            pltpu.VMEM(mass.shape, BF16),
            pltpu.VMEM(classes.shape[::-1], jnp.int32),
            pltpu.VMEM(routes.shape[::-1], jnp.int32),
            pltpu.VMEM((1, rays), jnp.int32),
            pltpu.VMEM(fit_table.shape[::-1], F32),
            pltpu.SMEM((1, site_phase.shape[0]), F32),
            pltpu.VMEM((PLANES, cells, slot_cols // PLANES), BF16),
            pltpu.VMEM((cells, levels), BF16),
            pltpu.VMEM((levels, cells), F32),
            pltpu.VMEM((blocks * cols, levels), F32),
            pltpu.VMEM((slot_cols, levels), F32),
            pltpu.VMEM((n, chunk, levels), BF16),
            pltpu.VMEM((n, 1, 128), F32),
            pltpu.VMEM((n, chunk, levels), BF16),
            pltpu.VMEM((n, 1, 128), F32),
            pltpu.VMEM((2, rays), F32),
            pltpu.VMEM((n, 2, rays), F32),
            pltpu.VMEM((3, 8, cells), F32),
            pltpu.SemaphoreType.DMA((PLANES + 7,)),
            pltpu.SemaphoreType.DMA((3,)),
            pltpu.SemaphoreType.DMA((PLANES,)),
            pltpu.SemaphoreType.DMA((PLANES,)),
            pltpu.SemaphoreType.DMA,
        ],
        compiler_params=pltpu.CompilerParams(
            collective_id=0, has_side_effects=True, vmem_limit_bytes=56 * 1024 * 1024
        ),
    )(
        mass, classes.T, routes.T, ray_site.reshape(1, rays), fit_table.T, site_phase.reshape(1, -1),
        beam_weight.reshape(cells, slot_cols), vertical_weight.reshape(cells, levels),
    )
    return pl.pallas_call(
        finish,
        out_shape=(jax.ShapeDtypeStruct((gates, rays), F32),) * 2,
        in_specs=[vmem, vmem],
        out_specs=(vmem, vmem),
    )(refl, phase)


def solution(mesh):
    placed = (
        P(("grp", "rng"), None, None),
        P(("grp", "rng"), None),
        P(("grp", "rng"), None),
        P(("grp", "rng"), None, None),
        P(("grp", "rng"), None, None),
        P("grp"),
        P(),
        P("grp"),
    )
    return jax.shard_map(
        local,
        mesh=mesh,
        in_specs=placed,
        out_specs=(P(("grp", "rng"), None), P(("grp", "rng"), None)),
        check_vma=False,
    )
```

time: 33.1 us -> 25.2 us (0.76)
  local copies, waits for them, and re-layouts: 6.73 us -> 0 us
  Pallas kernels: 25.3 us -> 24.4 us
    unnamed x5 -> x0, local copies, waits for them, and re-layouts: 6.73 us -> none
    pallas_call x1, Pallas kernels: 25.3 us -> 23 us  [local(): pl.pallas_call(functools.partial(kernel, n, cap), out_shape=(jax.ShapeDty...]
    pallas_call x0 -> x1, Pallas kernels: none -> 1.32 us  [local(): pl.pallas_call(finish, out_shape=(jax.ShapeDtypeStruct((gates, rays), F32...]
where the time goes in v2:
time: 25.2 us; the launch traced here: 25 us
  Pallas kernels  24.4 us (97%)
  between operations  0.64 us (3%)
    pallas_call x1, Pallas kernels, local(): pl.pallas_call(functools.partial(kernel, n, cap), out_shape=(jax.ShapeDty...  23 us
    pallas_call x1, Pallas kernels, local(): pl.pallas_call(finish, out_shape=(jax.ShapeDtypeStruct((gates, rays), F32...  1.32 us

profile of v2, /device:TPU:0, one launch (start us, length us, event | category | flops | bytes accessed | tf_op | source)
XLA Modules:
  0.0 25.0 jit_solution(5310253560495900336)
XLA Ops:
  0.6 23.0 %shard_map.95 = (f32[8,256]{1,0:T(8,128)}, f32[8,256]{1,0:T(8,128)}) custom-call(bf16[96,8,128]{2,1,0:T(8,128)(2,1)} %mass_hbm.1, s32[8,96]{1,0:T(8,128)} %bitcast.9, s32[2,96]{1,0:T(2,128)} %bitcast.11, s32[1,256]{1,0:T(1,128)} %bitcast.12, f32[6,16]{1,0:T(8,128)} %bitcast.10, f32[1,8]{1,0:T(1,128)} %bitcast.13, bf16[2048,1536]{1,0:T(8,128)(2,1)} %bitcast.7, ...), custom_call_target="tpu_custom_call" | custom-call | tf_op jit(solution)/shard_map/pallas_call | solution.py:273
  23.7 1.3 %shard_map.96 = (f32[8,256]{1,0:T(8,128)}, f32[8,256]{1,0:T(8,128)}) custom-call(f32[8,256]{1,0:T(8,128)} %get-tuple-element.4.refl_ref, f32[8,256]{1,0:T(8,128)} %get-tuple-element.5.phase_ref), custom_call_target="tpu_custom_call" | custom-call | tf_op jit(solution)/shard_map/pallas_call | solution.py:310

commit v3 on v2

--- a/solution.py
+++ b/solution.py
@@ -32,7 +32,7 @@
     refl_ref, phase_ref,
     mass_ref, classes_ref, routes_ref, ray_ref, table_ref, site_ref,
     weight, vertical, vertical_t, mass_f32, slots_f32, out_mass, out_class, in_mass, in_class,
-    out_total, in_total, beam_acc, load_sem, send_sem, mass_sem, class_sem, total_sem,
+    out_total, in_total, beam_acc, coeff_ref, load_sem, send_sem, mass_sem, class_sem, total_sem,
 ):
     me = lax.axis_index("rng")
     blocks, cols, levels = mass_ref.shape
@@ -49,11 +49,22 @@
 
     barrier = pltpu.get_barrier_semaphore()
 
-    def greet(i, _):
-        pl.semaphore_signal(barrier, 1, device_id=to((me + i) % n), device_id_type=MESH)
-        return 0
-
-    lax.fori_loop(1, n, greet, 0, unroll=n <= 16)
+    def each(z, start, act):
+        def step(i, _):
+            act(z * members + (place + i) % members)
+            return 0
+
+        lax.fori_loop(start, members, step, 0, unroll=n <= 16)
+
+    near = plane + 1 - 2 * (plane % 2)
+    far, last = (plane + 2) % PLANES, PLANES - 1 - plane
+    others = ((last, 0), (far, 0), (near, 0), (plane, 1))
+
+    def greet(target):
+        pl.semaphore_signal(barrier, 1, device_id=to(target), device_id_type=MESH)
+
+    for z, start in others:
+        each(z, start, greet)
 
     small = [
         pltpu.make_async_copy(source, target, load_sem.at[PLANES + 1 + i])
@@ -138,25 +149,12 @@
         part = ref.at[pl.ds(0, count)]
         pltpu.make_async_copy(part, part, sem).wait()
 
-    near = plane + 1 - 2 * (plane % 2)
-    far, last = (plane + 2) % PLANES, PLANES - 1 - plane
-    others = ((last, 0), (far, 0), (near, 0), (plane, 1))
-
-    def each(z, start, act):
-        def step(i, _):
-            act(z * members + (place + i) % members)
-            return 0
-
-        lax.fori_loop(start, members, step, 0, unroll=n <= 16)
-
-    def arrive(z, count):
-        wait_bytes(in_class, count, class_sem.at[z])
-        wait_bytes(in_mass, count, mass_sem.at[z])
-
     pl.semaphore_wait(barrier, n - 1)
-    for z, start in ((far, 0), (last, 0), (near, 0), (plane, 1)):
+    order = ((far, 0), (last, 0), (near, 0), (plane, 1))
+    for z, start in order:
+        each(z, start, lambda target: class_copy(target).start())
+    for z, start in order:
         each(z, start, lambda target: mass_copy(target).start())
-        each(z, start, lambda target: class_copy(target).start())
 
     in_mass[me] = out_mass[me]
     in_class[me] = out_class[me]
@@ -174,13 +172,16 @@
     unroll = unroll.astype(F32).astype(BF16)
     from_place = block_of(iota((members, depth), 1), chunk) == iota((members, depth), 0).astype(F32)
 
+    def fits_of(z):
+        class_grid = in_class[pl.ds(z * members, members)].reshape(members, 128)[:, :chunk]
+        class_row = dot(class_grid.astype(BF16), unroll)
+        class_row = jnp.sum(jnp.where(from_place, class_row, 0.0), axis=0, keepdims=True)
+        onehot = (class_row == iota((table_ref.shape[1], depth), 0).astype(F32)).astype(F32)
+        coeff_ref[z] = dot(table_ref[...], onehot, precision=lax.Precision.HIGHEST)
+
     def absorb(z, initial):
-        chosen = pl.ds(z * members, members)
-        class_grid = in_class[chosen].reshape(members, 128)[:, :chunk].astype(BF16)
-        class_row = jnp.sum(jnp.where(from_place, dot(class_grid, unroll), 0.0), axis=0, keepdims=True)
-        onehot = (class_row == iota((table_ref.shape[1], depth), 0).astype(F32)).astype(F32)
-        coeffs = dot(table_ref[...], onehot, precision=lax.Precision.HIGHEST)
-        mass_t = in_mass[chosen].reshape(depth, levels).astype(F32).T
+        coeffs = coeff_ref[z]
+        mass_t = in_mass[pl.ds(z * members, members)].reshape(depth, levels).astype(F32).T
         positive = mass_t > 0
         log_mass = jnp.log2(jnp.where(positive, mass_t, 1.0))
         fields_t = jnp.concatenate(
@@ -206,10 +207,15 @@
                 else:
                     beam_acc[j, :, cells] += part
 
-    arrive(plane, members - 1)
+    wait_bytes(in_class, members - 1, class_sem.at[plane])
+    for z in (near, far, last):
+        wait_bytes(in_class, members, class_sem.at[z])
+    for z in range(PLANES):
+        fits_of(z)
+    wait_bytes(in_mass, members - 1, mass_sem.at[plane])
     absorb(plane, True)
     for z in (near, far, last):
-        arrive(z, members)
+        wait_bytes(in_mass, members, mass_sem.at[z])
         absorb(z, False)
 
     gate_row = iota((gates, rays), 0)
@@ -294,6 +300,7 @@
             pltpu.VMEM((2, rays), F32),
             pltpu.VMEM((n, 2, rays), F32),
             pltpu.VMEM((3, 8, cells), F32),
+            pltpu.VMEM((PLANES, fit_table.shape[1], slot_cols // PLANES), F32),
             pltpu.SemaphoreType.DMA((PLANES + 7,)),
             pltpu.SemaphoreType.DMA((3,)),
             pltpu.SemaphoreType.DMA((PLANES,)),

time: 25.2 us -> 24.4 us (0.968)
  Pallas kernels: 24.4 us -> 23.5 us
    pallas_call x1, Pallas kernels: 23 us -> 22.2 us  [local(): pl.pallas_call(functools.partial(kernel, n, cap), out_shape=(jax.ShapeDty...]
where the time goes in v3:
time: 24.4 us; the launch traced here: 24.2 us
  Pallas kernels  23.5 us (96%)
  between operations  0.64 us (3%)
    pallas_call x1, Pallas kernels, local(): pl.pallas_call(functools.partial(kernel, n, cap), out_shape=(jax.ShapeDty...  22.2 us
    pallas_call x1, Pallas kernels, local(): pl.pallas_call(finish, out_shape=(jax.ShapeDtypeStruct((gates, rays), F32...  1.32 us

profile of v3, /device:TPU:0, one launch (start us, length us, event | category | flops | bytes accessed | tf_op | source)
XLA Modules:
  0.0 24.2 jit_solution(16425781774014901137)
XLA Ops:
  0.6 22.2 %shard_map.95 = (f32[8,256]{1,0:T(8,128)}, f32[8,256]{1,0:T(8,128)}) custom-call(bf16[96,8,128]{2,1,0:T(8,128)(2,1)} %mass_hbm.1, s32[8,96]{1,0:T(8,128)} %bitcast.9, s32[2,96]{1,0:T(2,128)} %bitcast.11, s32[1,256]{1,0:T(1,128)} %bitcast.12, f32[6,16]{1,0:T(8,128)} %bitcast.10, f32[1,8]{1,0:T(1,128)} %bitcast.13, bf16[2048,1536]{1,0:T(8,128)(2,1)} %bitcast.7, ...), custom_call_target="tpu_custom_call" | custom-call | tf_op jit(solution)/shard_map/pallas_call | solution.py:279
  22.8 1.3 %shard_map.96 = (f32[8,256]{1,0:T(8,128)}, f32[8,256]{1,0:T(8,128)}) custom-call(f32[8,256]{1,0:T(8,128)} %get-tuple-element.4.refl_ref, f32[8,256]{1,0:T(8,128)} %get-tuple-element.5.phase_ref), custom_call_target="tpu_custom_call" | custom-call | tf_op jit(solution)/shard_map/pallas_call | solution.py:317

commit v4 on v3

--- a/solution.py
+++ b/solution.py
@@ -138,10 +138,10 @@
             device_id=to(target), device_id_type=MESH,
         )
 
-    def total_copy(target):
+    def total_copy(target, distance):
         return pltpu.make_async_remote_copy(
             src_ref=out_total, dst_ref=in_total.at[me],
-            send_sem=send_sem.at[2], recv_sem=total_sem,
+            send_sem=send_sem.at[2 + distance], recv_sem=total_sem.at[plane],
             device_id=to(target), device_id_type=MESH,
         )
 
@@ -232,8 +232,13 @@
         for g in range(1, gates):
             sums = sums + beam_acc[j + 1, :, g * rays : (g + 1) * rays]
         out_total[j : j + 1, :] = jnp.sum(sums, axis=0, keepdims=True)
-    for z, start in others:
-        each(z, start, lambda target: total_copy(target).start())
+    for k in range(PLANES - 1, 0, -1):
+
+        @pl.when(plane + k < PLANES)
+        def _():
+            each(plane + k, 0, lambda target: total_copy(target, k).start())
+
+    each(plane, 1, lambda target: total_copy(target, 0).start())
 
     atten, spec_phase = gate_rows(1), gate_rows(2)
     in_total[me] = out_total[...]
@@ -253,14 +258,25 @@
     for i in range(site_ref.shape[1]):
         offsets = offsets + jnp.where(ray_ref[...] == i, site_ref[0, i], 0.0)
 
-    wait_bytes(in_total, n - 1, total_sem)
+    wait_bytes(in_total, members - 1, total_sem.at[plane])
+    for k in range(1, PLANES):
+
+        @pl.when(plane - k >= 0)
+        def _():
+            wait_bytes(in_total, members, total_sem.at[plane - k])
+
     sources = in_total[...]
     before = jnp.sum(jnp.where(iota(sources.shape, 0) < me, sources, 0.0), axis=0)
     step_len = 4.0 / (n * gates)
     refl_ref[...] = log_refl - 2.0 * step_len * (before[0:1] + atten_depth)
     phase_ref[...] = 2.0 * step_len * (before[1:2] + phase_sum) + offsets
 
-    wait_bytes(in_total, n - 1, send_sem.at[2])
+    wait_bytes(in_total, members - 1, send_sem.at[2])
+    for k in range(1, PLANES):
+
+        @pl.when(plane + k < PLANES)
+        def _():
+            wait_bytes(in_total, members, send_sem.at[2 + k])
 
 
 def finish(refl_ref, phase_ref, refl_out, phase_out):
@@ -302,10 +318,10 @@
             pltpu.VMEM((3, 8, cells), F32),
             pltpu.VMEM((PLANES, fit_table.shape[1], slot_cols // PLANES), F32),
             pltpu.SemaphoreType.DMA((PLANES + 7,)),
-            pltpu.SemaphoreType.DMA((3,)),
+            pltpu.SemaphoreType.DMA((2 + PLANES,)),
             pltpu.SemaphoreType.DMA((PLANES,)),
             pltpu.SemaphoreType.DMA((PLANES,)),
-            pltpu.SemaphoreType.DMA,
+            pltpu.SemaphoreType.DMA((PLANES,)),
         ],
         compiler_params=pltpu.CompilerParams(
             collective_id=0, has_side_effects=True, vmem_limit_bytes=56 * 1024 * 1024

time: 24.4 us -> 22.8 us (0.934)
  Pallas kernels: 23.5 us -> 22 us
    pallas_call x1, Pallas kernels: 22.2 us -> 20.6 us  [local(): pl.pallas_call(functools.partial(kernel, n, cap), out_shape=(jax.ShapeDty...]
where the time goes in v4:
time: 22.8 us; the launch traced here: 22.6 us
  Pallas kernels  22 us (96%)
  between operations  0.64 us (3%)
    pallas_call x1, Pallas kernels, local(): pl.pallas_call(functools.partial(kernel, n, cap), out_shape=(jax.ShapeDty...  20.6 us
    pallas_call x1, Pallas kernels, local(): pl.pallas_call(finish, out_shape=(jax.ShapeDtypeStruct((gates, rays), F32...  1.32 us

profile of v4, /device:TPU:0, one launch (start us, length us, event | category | flops | bytes accessed | tf_op | source)
XLA Modules:
  0.0 22.6 jit_solution(3558602726428744831)
XLA Ops:
  0.6 20.6 %shard_map.95 = (f32[8,256]{1,0:T(8,128)}, f32[8,256]{1,0:T(8,128)}) custom-call(bf16[96,8,128]{2,1,0:T(8,128)(2,1)} %mass_hbm.1, s32[8,96]{1,0:T(8,128)} %bitcast.9, s32[2,96]{1,0:T(2,128)} %bitcast.11, s32[1,256]{1,0:T(1,128)} %bitcast.12, f32[6,16]{1,0:T(8,128)} %bitcast.10, f32[1,8]{1,0:T(1,128)} %bitcast.13, bf16[2048,1536]{1,0:T(8,128)(2,1)} %bitcast.7, ...), custom_call_target="tpu_custom_call" | custom-call | tf_op jit(solution)/shard_map/pallas_call | solution.py:295
  21.3 1.3 %shard_map.96 = (f32[8,256]{1,0:T(8,128)}, f32[8,256]{1,0:T(8,128)}) custom-call(f32[8,256]{1,0:T(8,128)} %get-tuple-element.4.refl_ref, f32[8,256]{1,0:T(8,128)} %get-tuple-element.5.phase_ref), custom_call_target="tpu_custom_call" | custom-call | tf_op jit(solution)/shard_map/pallas_call | solution.py:333

commit v5 on v4

--- a/solution.py
+++ b/solution.py
@@ -150,7 +150,8 @@
         pltpu.make_async_copy(part, part, sem).wait()
 
     pl.semaphore_wait(barrier, n - 1)
-    order = ((far, 0), (last, 0), (near, 0), (plane, 1))
+    low = 2 - 2 * half
+    order = ((low, 0), (low + 1, 0), (near, 0), (plane, 1))
     for z, start in order:
         each(z, start, lambda target: class_copy(target).start())
     for z, start in order:
@@ -214,7 +215,7 @@
         fits_of(z)
     wait_bytes(in_mass, members - 1, mass_sem.at[plane])
     absorb(plane, True)
-    for z in (near, far, last):
+    for z in (near, 2 - half, 3 - 3 * half):
         wait_bytes(in_mass, members, mass_sem.at[z])
         absorb(z, False)
 

time: 22.8 us -> 22.8 us (level)
  no operation moved by 1% of the time
where the time goes in v5:
time: 22.8 us; the launch traced here: 22.6 us
  Pallas kernels  22 us (96%)
  between operations  0.64 us (3%)
    pallas_call x1, Pallas kernels, local(): pl.pallas_call(functools.partial(kernel, n, cap), out_shape=(jax.ShapeDty...  20.6 us
    pallas_call x1, Pallas kernels, local(): pl.pallas_call(finish, out_shape=(jax.ShapeDtypeStruct((gates, rays), F32...  1.32 us

profile of v5, /device:TPU:0, one launch (start us, length us, event | category | flops | bytes accessed | tf_op | source)
XLA Modules:
  0.0 22.6 jit_solution(2704527850822833717)
XLA Ops:
  0.6 20.6 %shard_map.95 = (f32[8,256]{1,0:T(8,128)}, f32[8,256]{1,0:T(8,128)}) custom-call(bf16[96,8,128]{2,1,0:T(8,128)(2,1)} %mass_hbm.1, s32[8,96]{1,0:T(8,128)} %bitcast.9, s32[2,96]{1,0:T(2,128)} %bitcast.11, s32[1,256]{1,0:T(1,128)} %bitcast.12, f32[6,16]{1,0:T(8,128)} %bitcast.10, f32[1,8]{1,0:T(1,128)} %bitcast.13, bf16[2048,1536]{1,0:T(8,128)(2,1)} %bitcast.7, ...), custom_call_target="tpu_custom_call" | custom-call | tf_op jit(solution)/shard_map/pallas_call | solution.py:296
  21.3 1.3 %shard_map.96 = (f32[8,256]{1,0:T(8,128)}, f32[8,256]{1,0:T(8,128)}) custom-call(f32[8,256]{1,0:T(8,128)} %get-tuple-element.4.refl_ref, f32[8,256]{1,0:T(8,128)} %get-tuple-element.5.phase_ref), custom_call_target="tpu_custom_call" | custom-call | tf_op jit(solution)/shard_map/pallas_call | solution.py:334
